TPU v7x, 128 devices: a whole 4x4x4 slice. The times are simulated.
128 devices in a mesh: loader: 4 (over y), enc: 32 (over x, z, core).
Axes of the slice: x: 4, y: 4, z: 4, core: 2. Of those that a mesh axis runs over, the one named last changes fastest.
Arguments:
- frames: bfloat16 [256, 128, 64, 128], P('loader', 'enc'), may hold values from -37 to 37
- clip_of_frame: int32 [256], P(('loader', 'enc')), may hold values from 0 to 7, never falling along the last dimension, each value on 1 to 128 neighbouring positions
- norm_gain: float32 [128], replicated, may hold values from 0.1 to 1.9
- norm_bias: float32 [128], replicated, may hold values from -3 to 3
- conv_weight: bfloat16 [3, 3, 3, 128, 128], replicated, may hold values from -0.109375 to 0.109375
- conv_bias: float32 [128], replicated, may hold values from -3 to 3
Outputs:
- latents: bfloat16 [256, 64, 32, 128], P('loader', 'enc')
Inputs may be any that keep to these rules, and one draw needn't show every extreme that they name: `clip_of_frame`: clip numbers never fall along the timeline; each clip has 1 to 128 frames, one exactly 128.
All inputs are finite; a program needn't handle non-finite values.
Results may differ from a plain program's by a relative error of at most 0.0013.
The roundings to bfloat16 on the way count: a program that leaves them out, or rounds other values in their place, can miss the bound.
Values may be sent and summed in bfloat16 or wider, within the bound.
A program may use at most 128 MiB of HBM per device.

v0:
```python
import jax
import jax.numpy as jnp
from jax import lax
from jax.sharding import PartitionSpec as P

GROUPS = 32


EPS = 1e-06


def entering(array, axis, combine, identity):
    peers, mine = (lax.axis_size(axis), lax.axis_index(axis))
    everything = jax.tree.map(lambda part: lax.all_gather(part, axis), array)
    start = jax.tree.map(
        lambda part, zero: jnp.broadcast_to(jnp.asarray(zero, part.dtype), part.shape),
        array,
        identity,
    )

    def lap(k, before):
        reached = k < mine
        new = combine(before, jax.tree.map(lambda part: part[k], everything))
        return jax.tree.map(lambda a, b: jnp.where(reached, a, b), new, before)

    return lax.fori_loop(0, peers, lap, start)


def passed_along(block, axis, distance):
    devices = range(lax.axis_size(axis))
    route = [(i - distance, i) for i in devices if i - distance in devices]
    return lax.ppermute(block, axis, route)


def group_sums(block):
    values = block.astype(jnp.float32)
    tlen = block.shape[0]
    per_group = block.shape[3] // GROUPS
    first = jnp.sum(values, axis=(1, 2)).reshape(tlen, GROUPS, per_group).sum(-1)
    second = jnp.sum(values * values, axis=(1, 2)).reshape(tlen, GROUPS, per_group).sum(-1)
    return (first, second)


def local_prefix(ids, first, second):
    position = jnp.arange(ids.shape[0])
    member = ((position[None, :] <= position[:, None]) & (ids[None, :] == ids[:, None])).astype(
        jnp.float32
    )
    run_first = jnp.dot(member, first, precision=lax.Precision.HIGHEST)
    run_second = jnp.dot(member, second, precision=lax.Precision.HIGHEST)
    run_count = jnp.sum(member, axis=1)
    summary = (
        ids[0].astype(jnp.float32),
        ids[-1].astype(jnp.float32),
        (ids[0] != ids[-1]).astype(jnp.float32),
        run_first[-1],
        run_second[-1],
        run_count[-1],
    )
    return (run_first, run_second, run_count, summary)


def chain_combine(earlier, later):
    a_first, a_last, a_reset, a_one, a_two, a_count = earlier
    b_first, b_last, b_reset, b_one, b_two, b_count = later
    joined = (b_reset == 0.0) & (b_first == a_last)
    one = jnp.where(joined, a_one + b_one, b_one)
    two = jnp.where(joined, a_two + b_two, b_two)
    count = jnp.where(joined, a_count + b_count, b_count)
    reset = jnp.maximum(jnp.maximum(a_reset, b_reset), (b_first != a_last).astype(jnp.float32))
    merged = (a_first, b_last, reset, one, two, count)
    a_none = a_first < 0.0
    b_none = b_first < 0.0
    return tuple(
        (
            jnp.where(b_none, x_a, jnp.where(a_none, x_b, x_m))
            for x_a, x_b, x_m in zip(earlier, later, merged)
        )
    )


def empty_summary():
    return (
        jnp.float32(-1.0),
        jnp.float32(-1.0),
        jnp.float32(0.0),
        jnp.zeros((GROUPS,), jnp.float32),
        jnp.zeros((GROUPS,), jnp.float32),
        jnp.float32(0.0),
    )


def normalize(block, ids, run_first, run_second, run_count, prefix, cells, norm_gain, norm_bias):
    match = (ids.astype(jnp.float32) == prefix[1]).astype(jnp.float32)
    one = run_first + match[:, None] * prefix[3]
    two = run_second + match[:, None] * prefix[4]
    count = run_count + match * prefix[5]
    per_group = block.shape[3] // GROUPS
    per = count * cells
    mean = one / per[:, None]
    var = two / per[:, None] - mean * mean
    inverse = lax.rsqrt(var + EPS)
    mean_c = jnp.repeat(mean, per_group, axis=1)
    inverse_c = jnp.repeat(inverse, per_group, axis=1)
    scaled = (block.astype(jnp.float32) - mean_c[:, None, None, :]) * (
        inverse_c[:, None, None, :] * norm_gain
    ) + norm_bias
    return jax.nn.silu(scaled).astype(jnp.bfloat16)


def last_two(act, ids):
    keep = jnp.stack([(ids[-2] == ids[-1]).astype(jnp.bfloat16), jnp.ones((), jnp.bfloat16)])
    return act * keep[:, None, None, None]


def conv_block(ext, ids_ext, conv_weight, conv_bias):
    tlen = ext.shape[0] - 2
    out_rows = (ext.shape[1] - 1) // 2
    out_cols = ext.shape[2] // 2
    chans = ext.shape[3]
    padded = jnp.pad(ext, ((0, 0), (0, 0), (1, 0), (0, 0)))
    stacked = jnp.concatenate(
        [padded[:, :, k : k + 2 * out_cols - 1 : 2, :] for k in range(3)], axis=-1
    )
    taps = conv_weight.reshape(3, 3, 3 * chans, chans)
    total = jnp.zeros((tlen, out_rows, out_cols, chans), jnp.float32)
    for kt in range(3):
        keep = (ids_ext[kt : kt + tlen] == ids_ext[2:]).astype(jnp.float32)
        partial_sum = jnp.zeros((tlen, out_rows, out_cols, chans), jnp.float32)
        for kh in range(3):
            piece = stacked[kt : kt + tlen, kh : kh + 2 * out_rows - 1 : 2]
            partial_sum = partial_sum + jnp.einsum(
                "thwk,kc->thwc", piece, taps[kt, kh], preferred_element_type=jnp.float32
            )
        total = total + keep[:, None, None, None] * partial_sum
    return (total + conv_bias).astype(jnp.bfloat16)


def local(frames, clip_of_frame, norm_gain, norm_bias, conv_weight, conv_bias):
    per_group = frames.shape[3] // GROUPS
    slab = lax.all_to_all(frames, "enc", split_axis=0, concat_axis=1, tiled=True)
    first, second = group_sums(slab)
    run_first, run_second, run_count, summary = local_prefix(clip_of_frame, first, second)
    prefix = entering(summary, ("loader", "enc"), chain_combine, empty_summary())
    cells = slab.shape[1] * slab.shape[2] * per_group
    act = normalize(
        slab, clip_of_frame, run_first, run_second, run_count, prefix, cells, norm_gain, norm_bias
    )
    rim = passed_along(last_two(act, clip_of_frame), ("loader", "enc"), 1)
    ext = jnp.concatenate([rim, act], axis=0)
    ext = jnp.pad(ext, ((0, 0), (1, 0), (0, 0), (0, 0)))
    ids_ext = jnp.concatenate(
        [jnp.stack([prefix[1], prefix[1]]), clip_of_frame.astype(jnp.float32)]
    )
    encoded = conv_block(ext, ids_ext, conv_weight, conv_bias)
    return lax.all_to_all(encoded, "enc", split_axis=1, concat_axis=0, tiled=True)


def solution(mesh):
    placed = (P("loader", "enc", None, None), P(("loader", "enc")), P(), P(), P(), P())
    return jax.shard_map(
        local, mesh=mesh, in_specs=placed, out_specs=P("loader", "enc", None, None), check_vma=False
    )
```

profile of v0, /device:TPU:1, one launch (start us, length us, event | category | flops | bytes accessed | tf_op | source)
XLA Modules:
  0.0 1392.8 jit_solution(2613681363177953140)
XLA Ops:
  0.0 9.6 all-to-all-start
  12.4 105.9 %all-reduce.6 = (f32[128]{0:T(128)S(1)}, f32[128]{0:T(128)S(1)}, f32[128]{0:T(128)S(1)}, f32[128]{0:T(128)S(1)}) all-reduce(f32[128]{0:T(128)S(1)} %convert_dynamic-update-slice_fusion.1, f32[128]{0:T(128)S(1)} %convert_dynamic-update-slice_fusion, f32[128]{0:T(128)S(1)} %fusion.25, ...), channel_id=1, replica_groups=mesh['loader'=4,'enc'=32] {'loader','enc'}, use_global_device_ids=true, to_apply=%add.2 | all-reduce | flops 512 | bytes 4096
  118.4 6.5 copy.14
  124.9 3.2 bitcast_convert_fusion
  128.2 1.1 fusion.3
  129.9 29.4 %all-gather = f32[128,1,32]{2,1,0:T(1,128)S(1)} all-gather(f32[1,1,32]{2,1,0:T(1,128)S(1)} %slice_bitcast_fusion.19), channel_id=1, replica_groups=mesh['loader'=4,'enc'=32] {'loader','enc'}, dimensions={0}, use_global_device_ids=true | all-gather | bytes 16512 | tf_op jit(solution)/shard_map/all_gather | solution.py:14
  159.3 29.5 %all-gather.1 = f32[128,1,32]{2,1,0:T(1,128)S(1)} all-gather(f32[1,1,32]{2,1,0:T(1,128)S(1)} %slice_bitcast_fusion.18), channel_id=1, replica_groups=mesh['loader'=4,'enc'=32] {'loader','enc'}, dimensions={0}, use_global_device_ids=true | all-gather | bytes 16512 | tf_op jit(solution)/shard_map/all_gather | solution.py:14
  188.8 976.4 %while.22 = (s32[]{:T(128)}, f32[]{:T(128)}, f32[]{:T(128)}, f32[32]{0:T(128)S(1)}, f32[32]{0:T(128)S(1)}, /*index=5*/f32[]{:T(128)}, s32[]{:T(128)}, f32[128]{0...) while((s32[]{:T(128)}, f32[]{:T(128)}, f32[]{:T(128)}, ...), condition=%wide.region_6.7_spmd.clone, body=%wide.region_5.6_spmd.clone.sunk | while | flops 403 | bytes 1176 | solution.py:26
  1165.8 5.4 broadcast_multiply_fusion
  1171.2 2.5 collective-permute-start
  1173.8 45.2 %collective-permute-done = bf16[2,128,64,128]{3,2,1,0:T(8,128)(2,1)S(1)} collective-permute-done((bf16[2,128,64,128]{3,2,1,0:T(8,128)(2,1)S(1)}, bf16[2,128,64,128]{3,2,1,0:T(8,128)(2,1)S(1)}, u32[]{:S(2)}, u32[]{:S(2)}) %collective-permute-start) | collective-permute-done | bytes 4194336 | tf_op jit(solution)/shard_map/ppermute | solution.py:32
  1219.0 2.1 fusion.2
  1221.2 7.6 pad.9
  1228.8 40.5 %slice.93 = bf16[4,129,32,128]{3,2,1,0:T(8,128)(2,1)} slice(bf16[4,129,65,128]{3,2,1,0:T(8,128)(2,1)} %pad.9), slice={[0:4:1], [0:129:1], [2:65:2], [0:128:1]} | slice | bytes 8454144 | tf_op jit(solution)/shard_map/slice | solution.py:123
  1269.3 40.3 %slice.92 = bf16[4,129,32,128]{3,2,1,0:T(8,128)(2,1)} slice(bf16[4,129,65,128]{3,2,1,0:T(8,128)(2,1)} %pad.9), slice={[0:4:1], [0:129:1], [1:64:2], [0:128:1]} | slice | bytes 8454144 | tf_op jit(solution)/shard_map/slice | solution.py:123
  1309.5 40.2 %slice.91 = bf16[4,129,32,128]{3,2,1,0:T(8,128)(2,1)} slice(bf16[4,129,65,128]{3,2,1,0:T(8,128)(2,1)} %pad.9), slice={[0:4:1], [0:129:1], [0:63:2], [0:128:1]} | slice | bytes 8454144 | tf_op jit(solution)/shard_map/slice | solution.py:123
  1349.7 6.5 pad_maximum_fusion
  1356.2 1.0 fusion.6
  1358.2 1.0 fusion.10
  1360.2 1.0 fusion.14
  1363.1 1.0 fusion.20
  1364.1 2.5 add_convert_fusion
  1366.8 24.9 %all_to_all.27 = bf16[2,64,32,128]{3,2,0,1:T(8,128)(2,1)S(1)} all-to-all(bf16[2,64,32,128]{3,2,0,1:T(8,128)(2,1)S(1)} %copy.15), channel_id=1, replica_groups=mesh['loader'=4,'enc'=32] {'enc'}, dimensions={1} | all-to-all | bytes 2097152 | tf_op jit(solution)/shard_map/all_to_all | solution.py:156
  1391.7 1.1 copy.16
  (687 shorter events, 310.7 us)
Async XLA Ops:
  0.0 9.7 copy-start.1
  0.0 118.4 %all-to-all-start = ((bf16[64,4,64,128]{3,2,1,0:T(8,128)(2,1)}), bf16[64,4,64,128]{3,2,1,0:T(8,128)(2,1)}, u32[]{:S(2)}, u32[]{:S(2)}) async-start(bf16[64,4,64,128]{3,2,1,0:T(8,128)(2,1)} %param.8), calls=%async_computation | async-start | bytes 8388608 | tf_op jit(solution)/shard_map/all_to_all | solution.py:141
  128.1 1037.7 %copy-start.4 = (f32[128]{0:T(128)S(1)}, f32[128]{0:T(128)}, u32[]{:S(2)}) copy-start(f32[128]{0:T(128)} %param.10) | copy-start | bytes 1540
  128.1 1037.7 %copy-start.3 = (f32[128]{0:T(128)S(1)}, f32[128]{0:T(128)}, u32[]{:S(2)}) copy-start(f32[128]{0:T(128)} %param.11) | copy-start | bytes 1540
  1171.2 47.8 %collective-permute-start = (bf16[2,128,64,128]{3,2,1,0:T(8,128)(2,1)S(1)}, bf16[2,128,64,128]{3,2,1,0:T(8,128)(2,1)S(1)}, u32[]{:S(2)}, u32[]{:S(2)}) collective-permute-start(bf16[2,128,64,128]{3,2,1,0:T(8,128)(2,1)S(1)} %get-tuple-element.300), channel_id=1, source_target_pairs={{0,1},{1,2},{2,3},{3,4},{4,5},{5,6},{6,7},{7,8},{8,9},{9,10},{10,1... | collective-permute-start | bytes 12582920 | tf_op jit(solution)/shard_map/ppermute | solution.py:32
  1349.7 6.5 copy-start
  1362.2 2.0 copy-start.2
where the time goes:
time: 1410 us; the launch traced here: 1390 us
  loops' own time  672 us (48%)
  local copies, waits for them, and re-layouts  439 us (31%)
  blocking collectives  190 us (13%)
  waiting for transfers between devices  45.2 us (3%)
  other arithmetic  22.3 us (2%)
    another operation x1, loops' own time, entering(): return lax.fori_loop(0, peers, lap, start)  672 us
    dynamic_slice x512, local copies, waits for them, and re-layouts, lap(): new = combine(before, jax.tree.map(lambda part: part[k], everything))  301 us
    slice x3, local copies, waits for them, and re-layouts, conv_block(): padded[:, :, k:k + 2 * out_cols - 1:2, :]  121 us
    unnamed x1, blocking collectives  106 us
    all_gather x2, blocking collectives, entering(): everything = jax.tree.map(lambda part: lax.all_gather(part, axis), array)  58.8 us
    ppermute x1, waiting for transfers between devices, passed_along(): return lax.ppermute(block, axis, route)  45.2 us
  transfers between devices with their start and end apart: 2, of which 1 were waited for; matrix products, arithmetic and copies ran while one was open for 0% of the time, Pallas kernels for 0%

commit v1 on v0

v1 whole, which is shorter than its diff:
```python
import functools

import jax
import jax.numpy as jnp
from jax import lax
from jax.experimental import pallas as pl
from jax.experimental.pallas import tpu as pltpu
from jax.sharding import PartitionSpec as P

MESH = pl.DeviceIdType.MESH
EPS = 1e-06
GROUP = 4
LOADERS, NX, NK = 4, 4, 8
CHUNK = 8


def spread(values, lane, at):
    only = jnp.where(lane % GROUP == at, values, 0.0)
    width = values.shape[1]
    total = only
    for other in range(GROUP):
        if other != at:
            total = total + pltpu.roll(only, (other - at) % width, axis=1)
    return total


def kernel(
    frames, clips, gain, bias, weight, conv_bias, out,
    x, act, tmp, w, part, gath1, sum1, gath2, sum2, table, scale, shift, keep1, keep2, obuf,
    ids_s, gain_v, bias_v, cbias_v,
    load_sem, small_sem, w_sem, out_sem, send_sem, recv1, recv2, recv3, recvh,
):
    frames_n, rows, cols, chans = frames.shape
    chunks = frames_n // CHUNK
    half = cols // 2
    l, e = lax.axis_index("loader"), lax.axis_index("enc")
    xi, k = e // NK, e % NK
    encs = NX * NK
    l_next, l_prev = (l + 1) % LOADERS, (l + LOADERS - 1) % LOADERS
    e_next, e_prev = (e + 1) % encs, (e + encs - 1) % encs

    loads = []
    for i in range(chunks):
        loads.append(
            pltpu.make_async_copy(
                frames.at[pl.ds(i * CHUNK, CHUNK)],
                x.at[pl.ds(2 + i * CHUNK, CHUNK), pl.ds(1, rows)],
                load_sem.at[i],
            )
        )
        loads[-1].start()
    smalls = [
        pltpu.make_async_copy(clips, ids_s, small_sem.at[0]),
        pltpu.make_async_copy(gain, gain_v, small_sem.at[1]),
        pltpu.make_async_copy(bias, bias_v, small_sem.at[2]),
        pltpu.make_async_copy(conv_bias, cbias_v, small_sem.at[3]),
    ]
    for copy in smalls:
        copy.start()

    barrier = pltpu.get_barrier_semaphore()

    def tell(device):
        pl.semaphore_signal(barrier, inc=1, device_id=device, device_id_type=MESH)

    partners8 = [(l, NK * xi + (k + i) % NK) for i in range(1, NK)]
    partners16 = [
        ((l + a) % LOADERS, NK * ((xi + b) % NX) + k)
        for a in range(LOADERS)
        for b in range(NX)
        if (a, b) != (0, 0)
    ]
    for device in partners8 + partners16 + [(l, e_prev), (l_prev, e_prev)]:
        tell(device)

    weights = [
        pltpu.make_async_copy(weight.at[:, :, 1], w.at[:, :, pl.ds(0, chans), pl.ds(0, chans)], w_sem.at[0]),
        pltpu.make_async_copy(weight.at[:, :, 2], w.at[:, :, pl.ds(chans, chans), pl.ds(0, chans)], w_sem.at[1]),
        pltpu.make_async_copy(weight.at[:, :, 0], w.at[:, :, pl.ds(chans, chans), pl.ds(chans, chans)], w_sem.at[2]),
    ]
    for copy in weights:
        copy.start()
    w[:, :, :chans, chans:] = jnp.zeros((3, 3, chans, chans), jnp.bfloat16)

    lane8 = lax.broadcasted_iota(jnp.int32, (CHUNK, chans), 1)
    row8 = lax.broadcasted_iota(jnp.int32, (CHUNK, chans), 0)
    smalls[0].wait()
    id_a, id_b = ids_s[0].astype(jnp.float32), ids_s[1].astype(jnp.float32)
    for i in range(chunks):
        loads[i].wait()
        values = x[pl.ds(2 + i * CHUNK, CHUNK), pl.ds(1, rows)].astype(jnp.float32)
        first = jnp.sum(values, axis=(1, 2))
        second = jnp.sum(values * values, axis=(1, 2))
        for by in (1, 2):
            first = first + pltpu.roll(first, chans - by, axis=1)
            second = second + pltpu.roll(second, chans - by, axis=1)
        second = pltpu.roll(second, 1, axis=1)
        ident = jnp.where(
            row8 + i * CHUNK == 2 * e, id_a, jnp.where(row8 + i * CHUNK == 2 * e + 1, id_b, 0.0)
        )
        role = lane8 % GROUP
        part[i] = jnp.where(
            role == 0, first, jnp.where(role == 1, second, jnp.where(role == 2, ident, 0.0))
        )

    pl.semaphore_wait(barrier, 24)

    def send(src, dst, at, recv, device):
        copy = pltpu.make_async_remote_copy(
            src_ref=src, dst_ref=dst, send_sem=send_sem.at[at], recv_sem=recv,
            device_id=device, device_id_type=MESH,
        )
        copy.start()
        return copy

    sent = []
    for i, device in enumerate(partners8):
        sent.append(
            send(part.at[(k + i + 1) % NK], gath1.at[k], i, recv1.at[k], device)
        )
    sent.append(
        send(frames.at[:, rows - 1], x.at[pl.ds(2, frames_n), 0], 29, recvh.at[0], (l, e_next))
    )
    sent.append(
        send(frames.at[pl.ds(frames_n - 2, 2)], x.at[pl.ds(0, 2), pl.ds(1, rows)], 30, recvh.at[1], (l_next, e))
    )
    sent.append(
        send(frames.at[pl.ds(frames_n - 2, 2), rows - 1], x.at[pl.ds(0, 2), 0], 31, recvh.at[2], (l_next, e_next))
    )

    def arrived(ref, sem):
        pltpu.make_async_copy(ref, ref, sem).wait()

    gath1[k] = part[k]
    for i in range(1, NK):
        slot = (k + i) % NK
        arrived(gath1.at[slot], recv1.at[slot])
    sum1[...] = jnp.sum(gath1[...], axis=0)

    mine = l * NX + xi
    for i, device in enumerate(partners16):
        sent.append(send(sum1, gath2.at[mine], 7 + i, recv2.at[mine], device))
    gath2[mine] = sum1[...]
    for a in range(LOADERS):
        for b in range(NX):
            if (a, b) != (0, 0):
                slot = ((l + a) % LOADERS) * NX + (xi + b) % NX
                arrived(gath2.at[slot], recv2.at[slot])
    for a in range(LOADERS):
        sum2[a] = gath2[a * NX] + gath2[a * NX + 1] + gath2[a * NX + 2] + gath2[a * NX + 3]

    for i, device in enumerate(partners8):
        sent.append(send(sum2, table.at[pl.ds(1, LOADERS), k], 22 + i, recv3.at[k], device))
    for a in range(LOADERS):
        table[1 + a, k] = sum2[a]
    table[0, NK - 1] = jnp.full((CHUNK, chans), -1.0, jnp.float32)
    for copy in smalls[1:]:
        copy.wait()
    for i in range(1, NK):
        slot = (k + i) % NK
        arrived(sum2, recv3.at[slot])

    total = LOADERS * frames_n
    lane_all = lax.broadcasted_iota(jnp.int32, (total, chans), 1) % GROUP
    everything = table[pl.ds(1, LOADERS)].reshape(total, chans)
    everything = jnp.where(lane_all == 3, 1.0, everything)
    count = frames_n + CHUNK
    here = jnp.concatenate([table[l, NK - 1], table[l + 1].reshape(frames_n, chans)], axis=0)
    lane = lax.broadcasted_iota(jnp.int32, (count, chans), 1)
    ids_col = spread(here, lane, 2)
    picks = jnp.where(lane == 2, 1.0, 0.0).astype(jnp.bfloat16)
    ids_row = lax.dot_general(
        picks, everything.astype(jnp.bfloat16), (((1,), (1,)), ((), ())), preferred_element_type=jnp.float32
    )
    at_col = lax.broadcasted_iota(jnp.int32, (count, total), 1)
    at_row = lax.broadcasted_iota(jnp.int32, (count, total), 0) + (l * frames_n - CHUNK)
    same = ids_row == jnp.concatenate([ids_col] * (total // chans), axis=1)
    member = jnp.where(same & (at_col <= at_row), 1.0, 0.0)
    run = jnp.dot(member, everything, precision=lax.Precision.HIGHEST, preferred_element_type=jnp.float32)
    per = jnp.maximum(spread(run, lane, 3), 1.0) * float(encs * rows * cols * GROUP)
    mean = spread(run, lane, 0) / per
    var = spread(run, lane, 1) / per - mean * mean
    times = lax.rsqrt(var + EPS) * gain_v[...]
    scale[...] = 0.5 * times
    shift[...] = 0.5 * (bias_v[...] - mean * times)
    tmp[0, pl.ds(0, count)] = ids_col
    own = tmp[0, pl.ds(CHUNK, frames_n)]
    keep1[...] = jnp.where(tmp[0, pl.ds(CHUNK - 1, frames_n)] == own, 1.0, 0.0)
    keep2[...] = jnp.where(tmp[0, pl.ds(CHUNK - 2, frames_n)] == own, 1.0, 0.0)

    def activate(frame, row, slot, live=None):
        h = x[frame, row].astype(jnp.float32) * scale[pl.ds(frame + CHUNK - 2, 1)] + shift[pl.ds(frame + CHUNK - 2, 1)]
        v = h + h * jnp.tanh(h)
        if live is not None:
            v = jnp.where(live, v, 0.0)
        tmp[slot, pl.ds(0, cols)] = v
        act[frame, row, :, pl.ds(0, chans)] = tmp[slot, pl.ds(0, half, stride=2)].astype(jnp.bfloat16)
        act[frame, row, :, pl.ds(chans, chans)] = tmp[slot, pl.ds(1, half, stride=2)].astype(jnp.bfloat16)

    positions = CHUNK * half
    inner = lax.broadcasted_iota(jnp.int32, (positions, chans), 0) % half

    def convolve(i, r):
        def product(kt):
            left = jnp.concatenate(
                [act[pl.ds(i * CHUNK + kt, CHUNK), 2 * r + kh].reshape(positions, 2 * chans) for kh in range(3)],
                axis=1,
            )
            return jnp.dot(left, w[kt].reshape(3 * 2 * chans, 2 * chans), preferred_element_type=jnp.float32)

        def kept(keep, value):
            mask = jnp.broadcast_to(keep[pl.ds(i * CHUNK, CHUNK)][:, None, :], (CHUNK, half, chans))
            mask = mask.reshape(positions, chans) > 0.5
            return jnp.concatenate(
                [jnp.where(mask, value[:, :chans], 0.0), jnp.where(mask, value[:, chans:], 0.0)], axis=1
            )

        both = product(2) + kept(keep1, product(1)) + kept(keep2, product(0))
        moved = jnp.where(inner == 0, 0.0, pltpu.roll(both[:, chans:], 1, axis=0))
        result = both[:, :chans] + moved + cbias_v[...]
        obuf[pl.ds(i * CHUNK, CHUNK), r] = result.astype(jnp.bfloat16).reshape(CHUNK, half, chans)

    def out_copy(i, r):
        return pltpu.make_async_copy(
            obuf.at[pl.ds(i * CHUNK, CHUNK), r], out.at[pl.ds(i * CHUNK, CHUNK), r], out_sem.at[r, i]
        )

    arrived(x.at[pl.ds(0, 2), pl.ds(1, rows)], recvh.at[1])
    for copy in weights:
        copy.wait()
    for frame in range(2):
        for row in range(1, rows + 1):
            activate(frame, row, frame * rows + row - 1)

    def lower(i, carry):
        for f in range(CHUNK):
            for row in range(1, rows + 1):
                activate(2 + i * CHUNK + f, row, f * rows + row - 1)
        convolve(i, 1)
        out_copy(i, 1).start()
        return carry

    lax.fori_loop(0, chunks, lower, 0)

    arrived(x.at[pl.ds(2, frames_n), 0], recvh.at[0])
    arrived(x.at[pl.ds(0, 2), 0], recvh.at[2])
    live = e > 0
    for frame in range(2):
        activate(frame, 0, frame, live)

    def upper(i, carry):
        for f in range(CHUNK):
            activate(2 + i * CHUNK + f, 0, f, live)
        convolve(i, 0)
        out_copy(i, 0).start()
        return carry

    lax.fori_loop(0, chunks, upper, 0)

    for copy in sent:
        copy.wait_send()
    for r in range(2):
        for i in range(chunks):
            out_copy(i, r).wait()


def local(frames, clip_of_frame, norm_gain, norm_bias, conv_weight, conv_bias):
    frames_n, rows, cols, chans = frames.shape
    half = cols // 2
    chunks = frames_n // CHUNK
    f32, bf16 = jnp.float32, jnp.bfloat16
    dma = pltpu.SemaphoreType.DMA
    return pl.pallas_call(
        kernel,
        out_shape=jax.ShapeDtypeStruct((frames_n, rows // 2, half, chans), bf16),
        in_specs=[pl.BlockSpec(memory_space=pl.ANY)] * 6,
        out_specs=pl.BlockSpec(memory_space=pl.ANY),
        scratch_shapes=[
            pltpu.VMEM((frames_n + 2, rows + 1, cols, chans), bf16),
            pltpu.VMEM((frames_n + 2, rows + 1, half, 2 * chans), bf16),
            pltpu.VMEM((CHUNK * rows, frames_n + CHUNK, chans), f32),
            pltpu.VMEM((3, 3, 2 * chans, 2 * chans), bf16),
            pltpu.VMEM((NK, CHUNK, chans), f32),
            pltpu.VMEM((NK, CHUNK, chans), f32),
            pltpu.VMEM((CHUNK, chans), f32),
            pltpu.VMEM((LOADERS * NX, CHUNK, chans), f32),
            pltpu.VMEM((LOADERS, CHUNK, chans), f32),
            pltpu.VMEM((LOADERS + 1, NK, CHUNK, chans), f32),
            pltpu.VMEM((frames_n + CHUNK, chans), f32),
            pltpu.VMEM((frames_n + CHUNK, chans), f32),
            pltpu.VMEM((frames_n, chans), f32),
            pltpu.VMEM((frames_n, chans), f32),
            pltpu.VMEM((frames_n, rows // 2, half, chans), bf16),
            pltpu.SMEM((2,), jnp.int32),
            pltpu.VMEM((1, chans), f32),
            pltpu.VMEM((1, chans), f32),
            pltpu.VMEM((1, chans), f32),
            dma((chunks,)),
            dma((4,)),
            dma((3,)),
            dma((2, chunks)),
            dma((32,)),
            dma((NK,)),
            dma((LOADERS * NX,)),
            dma((NK,)),
            dma((3,)),
        ],
        compiler_params=pltpu.CompilerParams(
            collective_id=0, has_side_effects=True, vmem_limit_bytes=48 * 1024 * 1024
        ),
    )(
        frames,
        clip_of_frame,
        norm_gain.reshape(1, chans),
        norm_bias.reshape(1, chans),
        conv_weight,
        conv_bias.reshape(1, chans),
    )


def solution(mesh):
    placed = (P("loader", "enc", None, None), P(("loader", "enc")), P(), P(), P(), P())
    return jax.shard_map(
        local, mesh=mesh, in_specs=placed, out_specs=P("loader", "enc", None, None), check_vma=False
    )
```

time: 1410 us -> 47.6 us (0.03); the launches traced: 1390 us -> 47.4 us
  loops' own time: 672 us -> 0 us
  local copies, waits for them, and re-layouts: 439 us -> 6.95 us
  blocking collectives: 190 us -> 0 us
  waiting for transfers between devices: 45.2 us -> 0 us
  Pallas kernels: 0 us -> 40.4 us
  other arithmetic: 22.3 us -> 0 us
    another operation x1 -> x0, loops' own time: 672 us -> none  [entering(): return lax.fori_loop(0, peers, lap, start)]
    dynamic_slice x512 -> x0, local copies, waits for them, and re-layouts: 301 us -> none  [lap(): new = combine(before, jax.tree.map(lambda part: part[k], everything))]
    slice x4 -> x0, local copies, waits for them, and re-layouts: 122 us -> none  [the longest x3 121 us: conv_block(): padded[:, :, k:k + 2 * out_cols - 1:2, :]]
    unnamed x1 -> x0, blocking collectives: 106 us -> none
    all_gather x2 -> x0, blocking collectives: 58.8 us -> none  [entering(): everything = jax.tree.map(lambda part: lax.all_gather(part, axis), array)]
    ppermute x1 -> x0, waiting for transfers between devices: 45.2 us -> none  [passed_along(): return lax.ppermute(block, axis, route)]
    pallas_call x0 -> x1, Pallas kernels: none -> 40.4 us  [local(): pl.pallas_call(kernel, out_shape=jax.ShapeDtypeStruct((frames_n, rows //...]
    all_to_all x1 -> x0, blocking collectives: 24.9 us -> none  [local(): lax.all_to_all(encoded, 'enc', split_axis=1, concat_axis=0, tiled=True)]
  transfers between devices with their start and end apart: 2 -> 0, of which waited for: 1 -> 0; matrix products, arithmetic and copies ran while one was open for 0% -> 0% of each run, Pallas kernels for 0% -> 0%
where the time goes in v1:
time: 47.6 us; the launch traced here: 47.4 us
  Pallas kernels  40.4 us (85%)
  local copies, waits for them, and re-layouts  6.95 us (15%)
    pallas_call x1, Pallas kernels, local(): pl.pallas_call(kernel, out_shape=jax.ShapeDtypeStruct((frames_n, rows //...  40.4 us
    unnamed x13, local copies, waits for them, and re-layouts  6.95 us

profile of v1, /device:TPU:1, one launch (start us, length us, event | category | flops | bytes accessed | tf_op | source)
XLA Modules:
  0.0 47.4 jit_solution(8636347927053151489)
XLA Ops:
  0.0 0.0 copy-start
  0.0 2.2 %copy-done = bf16[64,4,64,128]{3,2,1,0:T(8,128)(2,1)S(1)} copy-done((bf16[64,4,64,128]{3,2,1,0:T(8,128)(2,1)S(1)}, bf16[64,4,64,128]{3,2,1,0:T(8,128)(2,1)}, u32[]{:S(2)}) %copy-start) | copy-done | bytes 4194328
  2.2 0.0 copy-start.1
  2.2 1.2 %copy-done.1 = bf16[3,3,3,128,128]{4,3,2,1,0:T(8,128)(2,1)S(1)} copy-done((bf16[3,3,3,128,128]{4,3,2,1,0:T(8,128)(2,1)S(1)}, bf16[3,3,3,128,128]{4,3,2,1,0:T(8,128)(2,1)}, u32[]{:S(2)}) %copy-start.1) | copy-done | bytes 884760
  3.4 0.0 copy-start.2
  3.4 0.7 %copy-done.2 = s32[2]{0:T(128)S(1)} copy-done((s32[2]{0:T(128)S(1)}, s32[2]{0:T(128)}, u32[]{:S(2)}) %copy-start.2) | copy-done | bytes 32
  4.0 0.0 copy-start.3
  4.0 0.7 %copy-done.3 = f32[128]{0:T(128)S(1)} copy-done((f32[128]{0:T(128)S(1)}, f32[128]{0:T(128)}, u32[]{:S(2)}) %copy-start.3) | copy-done | bytes 536
  4.7 0.0 copy-start.4
  4.7 0.7 %copy-done.4 = f32[128]{0:T(128)S(1)} copy-done((f32[128]{0:T(128)S(1)}, f32[128]{0:T(128)}, u32[]{:S(2)}) %copy-start.4) | copy-done | bytes 536
  5.3 0.0 copy-start.5
  5.3 0.7 %copy-done.5 = f32[128]{0:T(128)S(1)} copy-done((f32[128]{0:T(128)S(1)}, f32[128]{0:T(128)}, u32[]{:S(2)}) %copy-start.5) | copy-done | bytes 536
  6.0 40.4 %shard_map.64 = bf16[64,2,32,128]{3,2,1,0:T(8,128)(2,1)S(1)} custom-call(bf16[64,4,64,128]{3,2,1,0:T(8,128)(2,1)S(1)} %copy-done, s32[2]{0:T(128)S(1)} %copy-done.2, f32[1,128]{1,0:T(1,128)S(1)} %bitcast.3, f32[1,128]{1,0:T(1,128)S(1)} %bitcast.4, bf16[3,3,3,128,128]{4,3,2,1,0:T(8,128)(2,1)S(1)} %copy-done.1, f32[1,128]{1,0:T(1,128)S(1)} %bitcast.5), custom_call_target="tpu_custom_call" | custom-call | tf_op jit(solution)/shard_map/pallas_call | solution.py:273
  46.4 1.0 %copy.8 = bf16[64,2,32,128]{3,2,1,0:T(8,128)(2,1)} copy(bf16[64,2,32,128]{3,2,1,0:T(8,128)(2,1)S(1)} %shard_map.64) | data formatting | bytes 2097152
Async XLA Ops:
  0.0 2.2 %copy-start = (bf16[64,4,64,128]{3,2,1,0:T(8,128)(2,1)S(1)}, bf16[64,4,64,128]{3,2,1,0:T(8,128)(2,1)}, u32[]{:S(2)}) copy-start(bf16[64,4,64,128]{3,2,1,0:T(8,128)(2,1)} %frames.1) | copy-start | bytes 12582916
  2.2 1.2 %copy-start.1 = (bf16[3,3,3,128,128]{4,3,2,1,0:T(8,128)(2,1)S(1)}, bf16[3,3,3,128,128]{4,3,2,1,0:T(8,128)(2,1)}, u32[]{:S(2)}) copy-start(bf16[3,3,3,128,128]{4,3,2,1,0:T(8,128)(2,1)} %weight.1) | copy-start | bytes 2654212
  3.4 0.7 %copy-start.2 = (s32[2]{0:T(128)S(1)}, s32[2]{0:T(128)}, u32[]{:S(2)}) copy-start(s32[2]{0:T(128)} %clips.1) | copy-start | bytes 28
  4.0 0.7 %copy-start.3 = (f32[128]{0:T(128)S(1)}, f32[128]{0:T(128)}, u32[]{:S(2)}) copy-start(f32[128]{0:T(128)} %param.8) | copy-start | bytes 1540
  4.7 0.7 %copy-start.4 = (f32[128]{0:T(128)S(1)}, f32[128]{0:T(128)}, u32[]{:S(2)}) copy-start(f32[128]{0:T(128)} %param.9) | copy-start | bytes 1540
  5.3 0.7 %copy-start.5 = (f32[128]{0:T(128)S(1)}, f32[128]{0:T(128)}, u32[]{:S(2)}) copy-start(f32[128]{0:T(128)} %param.11) | copy-start | bytes 1540

commit v2 on v1

v2 whole, which is shorter than its diff:
```python
import jax
import jax.numpy as jnp
from jax import lax
from jax.experimental import pallas as pl
from jax.experimental.pallas import tpu as pltpu
from jax.sharding import PartitionSpec as P

MESH = pl.DeviceIdType.MESH
EPS = 1e-06
GROUP = 4
LOADERS, NX, NZ, CORES = 4, 4, 4, 2
ENCS = NX * NZ * CORES
PIECE = 8
CHUNK = 8
EARLY, MIDDLE = 2, 8
BARRIER_AT = 4


def spread(values, lane, at):
    only = jnp.where(lane % GROUP == at, values, 0.0)
    width = values.shape[1]
    total = only
    for other in range(GROUP):
        if other != at:
            total = total + pltpu.roll(only, (other - at) % width, axis=1)
    return total


def kernel(
    frames, clips, gain, bias, weight, conv_bias, out,
    x, split, act, tmp, w, part, from_core, sum0, from_z, sum1, from_x, sum2, table,
    scale, shift, keep1, keep2, obuf, ids_s, gain_v, bias_v, cbias_v,
    load_sem, small_sem, w_sem, out_sem, send_sem, halo_send, recv_core, recv_z, recv_x, recv_y, recv_frames, recv_halo,
):
    frames_n, rows, cols, chans = frames.shape
    pieces, chunks = frames_n // PIECE, frames_n // CHUNK
    half = cols // 2
    l, e = lax.axis_index("loader"), lax.axis_index("enc")
    xi, z, c = e // (NZ * CORES), (e // CORES) % NZ, e % CORES

    def enc_at(xi, z, c):
        return (xi * NZ + z) * CORES + c

    l_next, l_prev = (l + 1) % LOADERS, (l + LOADERS - 1) % LOADERS
    e_next, e_prev = (e + 1) % ENCS, (e + ENCS - 1) % ENCS
    other_core = (l, enc_at(xi, z, 1 - c))
    along_z = [(l, enc_at(xi, (z + i) % NZ, c)) for i in range(1, NZ)]
    along_x = [(l, enc_at((xi + i) % NX, z, c)) for i in range(1, NX)]
    along_y = [((l + i) % LOADERS, e) for i in range(1, LOADERS)]

    barrier = pltpu.get_barrier_semaphore()
    senders = [other_core] + along_z + along_x + along_y + [(l, e_prev), (l_prev, e_prev)]
    for device in senders:
        pl.semaphore_signal(barrier, inc=1, device_id=device, device_id_type=MESH)

    loads = []
    for i in range(pieces):
        loads.append(
            pltpu.make_async_copy(
                frames.at[pl.ds(i * PIECE, PIECE)],
                x.at[pl.ds(2 + i * PIECE, PIECE), pl.ds(1, rows)],
                load_sem.at[i],
            )
        )
        loads[-1].start()
    smalls = [
        pltpu.make_async_copy(clips, ids_s, small_sem.at[0]),
        pltpu.make_async_copy(gain, gain_v, small_sem.at[1]),
        pltpu.make_async_copy(bias, bias_v, small_sem.at[2]),
        pltpu.make_async_copy(conv_bias, cbias_v, small_sem.at[3]),
    ]
    for copy in smalls:
        copy.start()
    weights = [
        pltpu.make_async_copy(weight.at[:, :, 1], w.at[:, :, pl.ds(0, chans), pl.ds(0, chans)], w_sem.at[0]),
        pltpu.make_async_copy(weight.at[:, :, 2], w.at[:, :, pl.ds(chans, chans), pl.ds(0, chans)], w_sem.at[1]),
        pltpu.make_async_copy(weight.at[:, :, 0], w.at[:, :, pl.ds(chans, chans), pl.ds(chans, chans)], w_sem.at[2]),
    ]
    for copy in weights:
        copy.start()

    def remote(src, dst, sent, recv, device):
        return pltpu.make_async_remote_copy(
            src_ref=src, dst_ref=dst, send_sem=sent, recv_sem=recv, device_id=device, device_id_type=MESH
        )

    def arrived(ref, sem):
        pltpu.make_async_copy(ref, ref, sem).wait()

    halos = [
        remote(
            frames.at[pl.ds(i * PIECE, PIECE), rows - 1],
            x.at[pl.ds(2 + i * PIECE, PIECE), 0],
            halo_send.at[i], recv_halo.at[i], (l, e_next),
        )
        for i in range(pieces)
    ]
    sent = [
        remote(frames.at[pl.ds(frames_n - 2, 2)], x.at[pl.ds(0, 2), pl.ds(1, rows)], send_sem.at[0], recv_frames.at[0], (l_next, e)),
        remote(frames.at[pl.ds(frames_n - 2, 2), rows - 1], x.at[pl.ds(0, 2), 0], send_sem.at[1], recv_frames.at[1], (l_next, e_next)),
    ]

    def start(copies):
        for copy in copies:
            copy.start()

    lane = lax.broadcasted_iota(jnp.int32, (PIECE, chans), 1)
    role = lane % GROUP
    sums = []
    for i in range(pieces):
        if i == BARRIER_AT:
            pl.semaphore_wait(barrier, len(senders))
            start(sent)
            start(halos[:EARLY])
        loads[i].wait()
        values = x[pl.ds(2 + i * PIECE, PIECE), pl.ds(1, rows)].astype(jnp.float32)
        first = jnp.sum(values, axis=(1, 2))
        second = jnp.sum(values * values, axis=(1, 2))
        for by in (1, 2):
            first = first + pltpu.roll(first, chans - by, axis=1)
            second = second + pltpu.roll(second, chans - by, axis=1)
        second = pltpu.roll(second, 1, axis=1)
        sums.append(jnp.where(role == 0, first, jnp.where(role == 1, second, 0.0)))
    smalls[0].wait()
    id_lane = (l % 2) * frames_n + 2 * e
    ids = jnp.where(
        lane == id_lane,
        (ids_s[0] + 1).astype(jnp.float32),
        jnp.where(lane == id_lane + 1, (ids_s[1] + 1).astype(jnp.float32), 0.0),
    )
    for core in range(CORES):
        for block in range(2):
            at = 4 * core + block
            part[core, pl.ds(block * PIECE, PIECE)] = sums[at] + pltpu.roll(sums[at + 2], 2, axis=1)
        part[core, pl.ds(2 * PIECE, PIECE)] = ids

    def exchange(value, slots, mine, sems, first_sem, devices):
        copies = [
            remote(value, slots.at[mine], send_sem.at[first_sem + i], sems.at[mine], device)
            for i, device in enumerate(devices)
        ]
        start(copies)
        return copies

    def collect(slots, mine, sems, count):
        for i in range(1, count):
            at = (mine + i) % count
            arrived(slots.at[at], sems.at[at])

    def divide(frame):
        for row in range(1, rows + 1):
            slot = row - 1
            tmp[slot] = x[frame, row].astype(jnp.float32)
            split[frame, row, :, pl.ds(0, chans)] = tmp[slot, pl.ds(0, half, stride=2)].astype(jnp.bfloat16)
            split[frame, row, :, pl.ds(chans, chans)] = tmp[slot, pl.ds(1, half, stride=2)].astype(jnp.bfloat16)

    def divide_some(first, last):
        def step(i, carry):
            for f in range(4):
                divide(2 + 4 * i + f)
            return carry

        lax.fori_loop(first, last, step, 0)

    to_core = remote(part.at[1 - c], from_core, send_sem.at[2], recv_core.at[0], other_core)
    to_core.start()
    sent.append(to_core)
    w[:, :, :chans, chans:] = jnp.zeros((3, 3, chans, chans), jnp.bfloat16)
    arrived(from_core, recv_core.at[0])
    sum0[...] = part[c] + from_core[...]
    sent += exchange(sum0, from_z, z, recv_z, 3, along_z)
    from_z[z] = sum0[...]
    steps = frames_n // 4
    divide_some(0, steps // 2)
    collect(from_z, z, recv_z, NZ)
    sum1[...] = jnp.sum(from_z[...], axis=0)
    sent += exchange(sum1, from_x, xi, recv_x, 6, along_x)
    from_x[xi] = sum1[...]
    start(halos[EARLY:MIDDLE])
    divide_some(steps // 2, steps)
    collect(from_x, xi, recv_x, NX)
    sum2[...] = jnp.sum(from_x[...], axis=0)
    sent += exchange(sum2, table.at[c], l, recv_y, 9, along_y)
    table[c, l] = sum2[...]
    start(halos[MIDDLE:])
    arrived(x.at[pl.ds(0, 2), pl.ds(1, rows)], recv_frames.at[0])
    for frame in range(2):
        divide(frame)
    collect(table.at[c], l, recv_y, LOADERS)
    to_core = remote(table.at[c], table.at[c], send_sem.at[12], recv_core.at[1], other_core)
    to_core.start()
    sent.append(to_core)
    for copy in smalls[1:] + weights:
        copy.wait()
    arrived(table.at[1 - c], recv_core.at[1])

    total, count = LOADERS * frames_n, frames_n + PIECE
    blocks = []
    for loader in range(LOADERS):
        for core in range(CORES):
            block = table[core, loader, pl.ds(0, 2 * PIECE)]
            blocks += [block, pltpu.roll(block, chans - 2, axis=1)]
    everything = jnp.concatenate(blocks, axis=0)
    lane_all = lax.broadcasted_iota(jnp.int32, (total, chans), 1) % GROUP
    everything = jnp.where(lane_all == 3, 1.0, everything)
    id_row = [table[0, loader, pl.ds(2 * PIECE, 1)] for loader in range(LOADERS)]
    id_row = jnp.concatenate([id_row[0] + id_row[1], id_row[2] + id_row[3]], axis=1)
    id_row = jnp.broadcast_to(id_row, (count, total))
    at_col = lax.broadcasted_iota(jnp.int32, (count, total), 1)
    at_row = lax.broadcasted_iota(jnp.int32, (count, total), 0) + (l * frames_n - PIECE)

    def id_before(by):
        return jnp.sum(jnp.where(at_col == at_row - by, id_row, 0.0), axis=1, keepdims=True)

    own = id_before(0)
    member = jnp.where((id_row == own) & (at_col <= at_row), 1.0, 0.0)
    run = jnp.dot(member, everything, precision=lax.Precision.HIGHEST, preferred_element_type=jnp.float32)
    lane_run = lax.broadcasted_iota(jnp.int32, (count, chans), 1)
    per = jnp.maximum(spread(run, lane_run, 3), 1.0) * float(ENCS * rows * cols * GROUP)
    mean = spread(run, lane_run, 0) / per
    var = spread(run, lane_run, 1) / per - mean * mean
    times = lax.rsqrt(var + EPS) * gain_v[...]
    scale[...] = 0.5 * times
    shift[...] = 0.5 * (bias_v[...] - mean * times)
    for keep, by in ((keep1, 1), (keep2, 2)):
        kept = jnp.where(id_before(by) == own, 1.0, 0.0)
        keep[...] = jnp.broadcast_to(kept[PIECE:], (frames_n, chans))

    def silu_of(value, frame):
        at = pl.ds(frame + PIECE - 2, 1)
        s, b = scale[at], shift[at]
        if value.shape[1] != chans:
            s, b = jnp.concatenate([s, s], axis=1), jnp.concatenate([b, b], axis=1)
        h = value.astype(jnp.float32) * s + b
        return h + h * jnp.tanh(h)

    def activate(frame):
        for row in range(1, rows + 1):
            act[frame, row] = silu_of(split[frame, row], frame).astype(jnp.bfloat16)

    def activate_halo(frame, slot):
        tmp[slot] = jnp.where(e > 0, silu_of(x[frame, 0], frame), 0.0)
        act[frame, 0, :, pl.ds(0, chans)] = tmp[slot, pl.ds(0, half, stride=2)].astype(jnp.bfloat16)
        act[frame, 0, :, pl.ds(chans, chans)] = tmp[slot, pl.ds(1, half, stride=2)].astype(jnp.bfloat16)

    positions = CHUNK * half
    inner = lax.broadcasted_iota(jnp.int32, (positions, chans), 0) % half

    def convolve(i, r):
        def product(kt):
            left = jnp.concatenate(
                [act[pl.ds(i * CHUNK + kt, CHUNK), 2 * r + kh].reshape(positions, 2 * chans) for kh in range(3)],
                axis=1,
            )
            return jnp.dot(left, w[kt].reshape(3 * 2 * chans, 2 * chans), preferred_element_type=jnp.float32)

        def kept(keep, value):
            mask = jnp.broadcast_to(keep[pl.ds(i * CHUNK, CHUNK)][:, None, :], (CHUNK, half, chans))
            mask = mask.reshape(positions, chans) > 0.5
            return jnp.concatenate(
                [jnp.where(mask, value[:, :chans], 0.0), jnp.where(mask, value[:, chans:], 0.0)], axis=1
            )

        both = product(2) + kept(keep1, product(1)) + kept(keep2, product(0))
        moved = jnp.where(inner == 0, 0.0, pltpu.roll(both[:, chans:], 1, axis=0))
        result = both[:, :chans] + moved + cbias_v[...]
        obuf[pl.ds(i * CHUNK, CHUNK), r] = result.astype(jnp.bfloat16).reshape(CHUNK, half, chans)

    def out_copy(i, r):
        return pltpu.make_async_copy(
            obuf.at[pl.ds(i * CHUNK, CHUNK), r], out.at[pl.ds(i * CHUNK, CHUNK), r], out_sem.at[r, i]
        )

    for frame in range(2):
        activate(frame)

    def lower(i, carry):
        for f in range(CHUNK):
            activate(2 + i * CHUNK + f)
        convolve(i, 1)
        out_copy(i, 1).start()
        return carry

    lax.fori_loop(0, chunks, lower, 0)

    arrived(x.at[pl.ds(0, 2), 0], recv_frames.at[1])
    for frame in range(2):
        activate_halo(frame, frame)

    def upper(i, carry):
        for j in range(CHUNK // PIECE):
            piece = i * (CHUNK // PIECE) + j
            arrived(x.at[pl.ds(2 + piece * PIECE, PIECE), 0], recv_halo.at[piece])
        for f in range(CHUNK):
            activate_halo(2 + i * CHUNK + f, f)
        convolve(i, 0)
        out_copy(i, 0).start()
        return carry

    lax.fori_loop(0, chunks, upper, 0)

    for copy in sent + halos:
        copy.wait_send()
    for r in range(2):
        for i in range(chunks):
            out_copy(i, r).wait()


def local(frames, clip_of_frame, norm_gain, norm_bias, conv_weight, conv_bias):
    frames_n, rows, cols, chans = frames.shape
    half = cols // 2
    pieces, chunks = frames_n // PIECE, frames_n // CHUNK
    f32, bf16 = jnp.float32, jnp.bfloat16
    dma = pltpu.SemaphoreType.DMA
    load = 3 * PIECE
    return pl.pallas_call(
        kernel,
        out_shape=jax.ShapeDtypeStruct((frames_n, rows // 2, half, chans), bf16),
        in_specs=[pl.BlockSpec(memory_space=pl.ANY)] * 6,
        out_specs=pl.BlockSpec(memory_space=pl.ANY),
        scratch_shapes=[
            pltpu.VMEM((frames_n + 2, rows + 1, cols, chans), bf16),
            pltpu.VMEM((frames_n + 2, rows + 1, half, 2 * chans), bf16),
            pltpu.VMEM((frames_n + 2, rows + 1, half, 2 * chans), bf16),
            pltpu.VMEM((CHUNK, cols, chans), f32),
            pltpu.VMEM((3, 3, 2 * chans, 2 * chans), bf16),
            pltpu.VMEM((CORES, load, chans), f32),
            pltpu.VMEM((load, chans), f32),
            pltpu.VMEM((load, chans), f32),
            pltpu.VMEM((NZ, load, chans), f32),
            pltpu.VMEM((load, chans), f32),
            pltpu.VMEM((NX, load, chans), f32),
            pltpu.VMEM((load, chans), f32),
            pltpu.VMEM((CORES, LOADERS, load, chans), f32),
            pltpu.VMEM((frames_n + PIECE, chans), f32),
            pltpu.VMEM((frames_n + PIECE, chans), f32),
            pltpu.VMEM((frames_n, chans), f32),
            pltpu.VMEM((frames_n, chans), f32),
            pltpu.VMEM((frames_n, rows // 2, half, chans), bf16),
            pltpu.SMEM((2,), jnp.int32),
            pltpu.VMEM((1, chans), f32),
            pltpu.VMEM((1, chans), f32),
            pltpu.VMEM((1, chans), f32),
            dma((pieces,)),
            dma((4,)),
            dma((3,)),
            dma((2, chunks)),
            dma((13,)),
            dma((pieces,)),
            dma((2,)),
            dma((NZ,)),
            dma((NX,)),
            dma((LOADERS,)),
            dma((2,)),
            dma((pieces,)),
        ],
        compiler_params=pltpu.CompilerParams(
            collective_id=0, has_side_effects=True, vmem_limit_bytes=60 * 1024 * 1024
        ),
    )(
        frames,
        clip_of_frame,
        norm_gain.reshape(1, chans),
        norm_bias.reshape(1, chans),
        conv_weight,
        conv_bias.reshape(1, chans),
    )


def solution(mesh):
    placed = (P("loader", "enc", None, None), P(("loader", "enc")), P(), P(), P(), P())
    return jax.shard_map(
        local, mesh=mesh, in_specs=placed, out_specs=P("loader", "enc", None, None), check_vma=False
    )
```

time: 47.6 us -> 36.5 us (0.77)
  Pallas kernels: 40.4 us -> 34.1 us
  local copies, waits for them, and re-layouts: 6.95 us -> 2.26 us
    pallas_call x1, Pallas kernels: 40.4 us -> 34.1 us  [local(): pl.pallas_call(kernel, out_shape=jax.ShapeDtypeStruct((frames_n, rows //...]
    unnamed x13 -> x1, local copies, waits for them, and re-layouts: 6.95 us -> 2.26 us
where the time goes in v2:
time: 36.5 us; the launch traced here: 36.3 us
  Pallas kernels  34.1 us (93%)
  local copies, waits for them, and re-layouts  2.26 us (6%)
    pallas_call x1, Pallas kernels, local(): pl.pallas_call(kernel, out_shape=jax.ShapeDtypeStruct((frames_n, rows //...  34.1 us
    unnamed x1, local copies, waits for them, and re-layouts  2.26 us

profile of v2, /device:TPU:1, one launch (start us, length us, event | category | flops | bytes accessed | tf_op | source)
XLA Modules:
  0.0 36.3 jit_solution(16952061645659207480)
XLA Ops:
  0.0 34.1 %shard_map.64 = bf16[64,2,32,128]{3,2,1,0:T(8,128)(2,1)} custom-call(bf16[64,4,64,128]{3,2,1,0:T(8,128)(2,1)} %frames.1, s32[2]{0:T(128)} %clips.1, f32[1,128]{1,0:T(1,128)} %bitcast.3, f32[1,128]{1,0:T(1,128)} %bitcast.4, bf16[3,3,3,128,128]{4,3,2,1,0:T(8,128)(2,1)} %weight.1, f32[1,128]{1,0:T(1,128)} %bitcast.5), custom_call_target="tpu_custom_call" | custom-call | tf_op jit(solution)/shard_map/pallas_call | solution.py:316
  34.1 2.3 %copy.8 = bf16[64,2,32,128]{3,2,1,0:T(8,128)(2,1)} copy(bf16[64,2,32,128]{3,2,1,0:T(8,128)(2,1)} %shard_map.64) | data formatting | bytes 2097152

commit v3 on v2

--- a/solution.py
+++ b/solution.py
@@ -266,44 +266,43 @@
         result = both[:, :chans] + moved + cbias_v[...]
         obuf[pl.ds(i * CHUNK, CHUNK), r] = result.astype(jnp.bfloat16).reshape(CHUNK, half, chans)
 
-    def out_copy(i, r):
-        return pltpu.make_async_copy(
-            obuf.at[pl.ds(i * CHUNK, CHUNK), r], out.at[pl.ds(i * CHUNK, CHUNK), r], out_sem.at[r, i]
-        )
+    def out_copy(r):
+        return pltpu.make_async_copy(obuf.at[:, r], out.at[:, r], out_sem.at[r])
+
+    def activate_chunk(i):
+        for f in range(CHUNK):
+            activate(2 + i * CHUNK + f)
 
     for frame in range(2):
         activate(frame)
-
-    def lower(i, carry):
+    activate_chunk(0)
+    for i in range(chunks):
+        if i + 1 < chunks:
+            activate_chunk(i + 1)
+        convolve(i, 1)
+    out_copy(1).start()
+
+    for piece in range(pieces):
+        arrived(x.at[pl.ds(2 + piece * PIECE, PIECE), 0], recv_halo.at[piece])
+    arrived(x.at[pl.ds(0, 2), 0], recv_frames.at[1])
+
+    def activate_halo_chunk(i):
         for f in range(CHUNK):
-            activate(2 + i * CHUNK + f)
-        convolve(i, 1)
-        out_copy(i, 1).start()
-        return carry
-
-    lax.fori_loop(0, chunks, lower, 0)
-
-    arrived(x.at[pl.ds(0, 2), 0], recv_frames.at[1])
+            activate_halo(2 + i * CHUNK + f, 2 + i * CHUNK + f)
+
     for frame in range(2):
         activate_halo(frame, frame)
-
-    def upper(i, carry):
-        for j in range(CHUNK // PIECE):
-            piece = i * (CHUNK // PIECE) + j
-            arrived(x.at[pl.ds(2 + piece * PIECE, PIECE), 0], recv_halo.at[piece])
-        for f in range(CHUNK):
-            activate_halo(2 + i * CHUNK + f, f)
+    activate_halo_chunk(0)
+    for i in range(chunks):
+        if i + 1 < chunks:
+            activate_halo_chunk(i + 1)
         convolve(i, 0)
-        out_copy(i, 0).start()
-        return carry
-
-    lax.fori_loop(0, chunks, upper, 0)
+    out_copy(0).start()
 
     for copy in sent + halos:
         copy.wait_send()
     for r in range(2):
-        for i in range(chunks):
-            out_copy(i, r).wait()
+        out_copy(r).wait()
 
 
 def local(frames, clip_of_frame, norm_gain, norm_bias, conv_weight, conv_bias):
@@ -322,7 +321,7 @@
             pltpu.VMEM((frames_n + 2, rows + 1, cols, chans), bf16),
             pltpu.VMEM((frames_n + 2, rows + 1, half, 2 * chans), bf16),
             pltpu.VMEM((frames_n + 2, rows + 1, half, 2 * chans), bf16),
-            pltpu.VMEM((CHUNK, cols, chans), f32),
+            pltpu.VMEM((frames_n + 2, cols, chans), f32),
             pltpu.VMEM((3, 3, 2 * chans, 2 * chans), bf16),
             pltpu.VMEM((CORES, load, chans), f32),
             pltpu.VMEM((load, chans), f32),
@@ -344,7 +343,7 @@
             dma((pieces,)),
             dma((4,)),
             dma((3,)),
-            dma((2, chunks)),
+            dma((2,)),
             dma((13,)),
             dma((pieces,)),
             dma((2,)),

time: 36.5 us -> 33.7 us (0.923)
  Pallas kernels: 34.1 us -> 31.3 us
    pallas_call x1, Pallas kernels: 34.1 us -> 31.3 us  [local(): pl.pallas_call(kernel, out_shape=jax.ShapeDtypeStruct((frames_n, rows //...]
where the time goes in v3:
time: 33.7 us; the launch traced here: 33.6 us
  Pallas kernels  31.3 us (93%)
  local copies, waits for them, and re-layouts  2.26 us (7%)
    pallas_call x1, Pallas kernels, local(): pl.pallas_call(kernel, out_shape=jax.ShapeDtypeStruct((frames_n, rows //...  31.3 us
    unnamed x1, local copies, waits for them, and re-layouts  2.26 us

profile of v3, /device:TPU:1, one launch (start us, length us, event | category | flops | bytes accessed | tf_op | source)
XLA Modules:
  0.0 33.6 jit_solution(8003132711833549831)
XLA Ops:
  0.0 31.3 %shard_map.64 = bf16[64,2,32,128]{3,2,1,0:T(8,128)(2,1)} custom-call(bf16[64,4,64,128]{3,2,1,0:T(8,128)(2,1)} %frames.1, s32[2]{0:T(128)} %clips.1, f32[1,128]{1,0:T(1,128)} %bitcast.3, f32[1,128]{1,0:T(1,128)} %bitcast.4, bf16[3,3,3,128,128]{4,3,2,1,0:T(8,128)(2,1)} %weight.1, f32[1,128]{1,0:T(1,128)} %bitcast.5), custom_call_target="tpu_custom_call" | custom-call | tf_op jit(solution)/shard_map/pallas_call | solution.py:315
  31.3 2.3 %copy.8 = bf16[64,2,32,128]{3,2,1,0:T(8,128)(2,1)} copy(bf16[64,2,32,128]{3,2,1,0:T(8,128)(2,1)} %shard_map.64) | data formatting | bytes 2097152

commit v4 on v3

--- a/solution.py
+++ b/solution.py
@@ -12,7 +12,7 @@
 ENCS = NX * NZ * CORES
 PIECE = 8
 CHUNK = 8
-EARLY, MIDDLE = 2, 8
+EARLY = 2
 BARRIER_AT = 4
 
 
@@ -28,9 +28,9 @@
 
 def kernel(
     frames, clips, gain, bias, weight, conv_bias, out,
-    x, split, act, tmp, w, part, from_core, sum0, from_z, sum1, from_x, sum2, table,
-    scale, shift, keep1, keep2, obuf, ids_s, gain_v, bias_v, cbias_v,
-    load_sem, small_sem, w_sem, out_sem, send_sem, halo_send, recv_core, recv_z, recv_x, recv_y, recv_frames, recv_halo,
+    x, split, act, tmp, w, part, from_chips, sum1, from_plane, table,
+    scale, shift, keep1, keep2, ids_s, gain_v, bias_v, cbias_v,
+    load_sem, small_sem, w_sem, send_sem, halo_send, recv_chips, recv_plane, recv_core, recv_frames, recv_halo,
 ):
     frames_n, rows, cols, chans = frames.shape
     pieces, chunks = frames_n // PIECE, frames_n // CHUNK
@@ -44,12 +44,13 @@
     l_next, l_prev = (l + 1) % LOADERS, (l + LOADERS - 1) % LOADERS
     e_next, e_prev = (e + 1) % ENCS, (e + ENCS - 1) % ENCS
     other_core = (l, enc_at(xi, z, 1 - c))
-    along_z = [(l, enc_at(xi, (z + i) % NZ, c)) for i in range(1, NZ)]
-    along_x = [(l, enc_at((xi + i) % NX, z, c)) for i in range(1, NX)]
-    along_y = [((l + i) % LOADERS, e) for i in range(1, LOADERS)]
+    column = [(i, j) for i in range(NZ) for j in range(CORES) if (i, j) != (0, 0)]
+    column_devices = [(l, enc_at(xi, (z + i) % NZ, (c + j) % CORES)) for i, j in column]
+    plane = [(i, j) for i in range(LOADERS) for j in range(NX) if (i, j) != (0, 0)]
+    plane_devices = [((l + i) % LOADERS, enc_at((xi + j) % NX, z, c)) for i, j in plane]
 
     barrier = pltpu.get_barrier_semaphore()
-    senders = [other_core] + along_z + along_x + along_y + [(l, e_prev), (l_prev, e_prev)]
+    senders = column_devices + plane_devices + [(l, e_prev), (l_prev, e_prev)]
     for device in senders:
         pl.semaphore_signal(barrier, inc=1, device_id=device, device_id_type=MESH)
 
@@ -132,20 +133,7 @@
         for block in range(2):
             at = 4 * core + block
             part[core, pl.ds(block * PIECE, PIECE)] = sums[at] + pltpu.roll(sums[at + 2], 2, axis=1)
-        part[core, pl.ds(2 * PIECE, PIECE)] = ids
-
-    def exchange(value, slots, mine, sems, first_sem, devices):
-        copies = [
-            remote(value, slots.at[mine], send_sem.at[first_sem + i], sems.at[mine], device)
-            for i, device in enumerate(devices)
-        ]
-        start(copies)
-        return copies
-
-    def collect(slots, mine, sems, count):
-        for i in range(1, count):
-            at = (mine + i) % count
-            arrived(slots.at[at], sems.at[at])
+        part[core, pl.ds(2 * PIECE, 1)] = ids[:1]
 
     def divide(frame):
         for row in range(1, rows + 1):
@@ -162,37 +150,37 @@
 
         lax.fori_loop(first, last, step, 0)
 
-    to_core = remote(part.at[1 - c], from_core, send_sem.at[2], recv_core.at[0], other_core)
-    to_core.start()
-    sent.append(to_core)
+    for n, ((i, j), device) in enumerate(zip(column, column_devices)):
+        sent.append(remote(part.at[(c + j) % CORES], from_chips.at[z, c], send_sem.at[2 + n], recv_chips.at[z, c], device))
+        sent[-1].start()
     w[:, :, :chans, chans:] = jnp.zeros((3, 3, chans, chans), jnp.bfloat16)
-    arrived(from_core, recv_core.at[0])
-    sum0[...] = part[c] + from_core[...]
-    sent += exchange(sum0, from_z, z, recv_z, 3, along_z)
-    from_z[z] = sum0[...]
+    from_chips[z, c] = part[c]
     steps = frames_n // 4
     divide_some(0, steps // 2)
-    collect(from_z, z, recv_z, NZ)
-    sum1[...] = jnp.sum(from_z[...], axis=0)
-    sent += exchange(sum1, from_x, xi, recv_x, 6, along_x)
-    from_x[xi] = sum1[...]
-    start(halos[EARLY:MIDDLE])
+    for i, j in column:
+        at = ((z + i) % NZ, (c + j) % CORES)
+        arrived(from_chips.at[at], recv_chips.at[at])
+    sum1[...] = jnp.sum(from_chips[...], axis=(0, 1))
+    for n, device in enumerate(plane_devices):
+        sent.append(remote(sum1, from_plane.at[l, xi], send_sem.at[9 + n], recv_plane.at[l, xi], device))
+        sent[-1].start()
+    from_plane[l, xi] = sum1[...]
+    start(halos[EARLY:])
     divide_some(steps // 2, steps)
-    collect(from_x, xi, recv_x, NX)
-    sum2[...] = jnp.sum(from_x[...], axis=0)
-    sent += exchange(sum2, table.at[c], l, recv_y, 9, along_y)
-    table[c, l] = sum2[...]
-    start(halos[MIDDLE:])
     arrived(x.at[pl.ds(0, 2), pl.ds(1, rows)], recv_frames.at[0])
     for frame in range(2):
         divide(frame)
-    collect(table.at[c], l, recv_y, LOADERS)
-    to_core = remote(table.at[c], table.at[c], send_sem.at[12], recv_core.at[1], other_core)
+    for i, j in plane:
+        at = ((l + i) % LOADERS, (xi + j) % NX)
+        arrived(from_plane.at[at], recv_plane.at[at])
+    for loader in range(LOADERS):
+        table[c, loader] = jnp.sum(from_plane[loader], axis=0)
+    to_core = remote(table.at[c], table.at[c], send_sem.at[24], recv_core.at[0], other_core)
     to_core.start()
     sent.append(to_core)
     for copy in smalls[1:] + weights:
         copy.wait()
-    arrived(table.at[1 - c], recv_core.at[1])
+    arrived(table.at[1 - c], recv_core.at[0])
 
     total, count = LOADERS * frames_n, frames_n + PIECE
     blocks = []
@@ -264,10 +252,7 @@
         both = product(2) + kept(keep1, product(1)) + kept(keep2, product(0))
         moved = jnp.where(inner == 0, 0.0, pltpu.roll(both[:, chans:], 1, axis=0))
         result = both[:, :chans] + moved + cbias_v[...]
-        obuf[pl.ds(i * CHUNK, CHUNK), r] = result.astype(jnp.bfloat16).reshape(CHUNK, half, chans)
-
-    def out_copy(r):
-        return pltpu.make_async_copy(obuf.at[:, r], out.at[:, r], out_sem.at[r])
+        out[pl.ds(i * CHUNK, CHUNK), r] = result.astype(jnp.bfloat16).reshape(CHUNK, half, chans)
 
     def activate_chunk(i):
         for f in range(CHUNK):
@@ -280,7 +265,6 @@
         if i + 1 < chunks:
             activate_chunk(i + 1)
         convolve(i, 1)
-    out_copy(1).start()
 
     for piece in range(pieces):
         arrived(x.at[pl.ds(2 + piece * PIECE, PIECE), 0], recv_halo.at[piece])
@@ -297,12 +281,9 @@
         if i + 1 < chunks:
             activate_halo_chunk(i + 1)
         convolve(i, 0)
-    out_copy(0).start()
 
     for copy in sent + halos:
         copy.wait_send()
-    for r in range(2):
-        out_copy(r).wait()
 
 
 def local(frames, clip_of_frame, norm_gain, norm_bias, conv_weight, conv_bias):
@@ -311,12 +292,12 @@
     pieces, chunks = frames_n // PIECE, frames_n // CHUNK
     f32, bf16 = jnp.float32, jnp.bfloat16
     dma = pltpu.SemaphoreType.DMA
-    load = 3 * PIECE
+    load = 2 * PIECE + 1
     return pl.pallas_call(
         kernel,
-        out_shape=jax.ShapeDtypeStruct((frames_n, rows // 2, half, chans), bf16),
+        out_shape=pltpu.VMEM((frames_n, rows // 2, half, chans), bf16),
         in_specs=[pl.BlockSpec(memory_space=pl.ANY)] * 6,
-        out_specs=pl.BlockSpec(memory_space=pl.ANY),
+        out_specs=pl.BlockSpec(memory_space=pltpu.VMEM),
         scratch_shapes=[
             pltpu.VMEM((frames_n + 2, rows + 1, cols, chans), bf16),
             pltpu.VMEM((frames_n + 2, rows + 1, half, 2 * chans), bf16),
@@ -324,18 +305,14 @@
             pltpu.VMEM((frames_n + 2, cols, chans), f32),
             pltpu.VMEM((3, 3, 2 * chans, 2 * chans), bf16),
             pltpu.VMEM((CORES, load, chans), f32),
+            pltpu.VMEM((NZ, CORES, load, chans), f32),
             pltpu.VMEM((load, chans), f32),
-            pltpu.VMEM((load, chans), f32),
-            pltpu.VMEM((NZ, load, chans), f32),
-            pltpu.VMEM((load, chans), f32),
-            pltpu.VMEM((NX, load, chans), f32),
-            pltpu.VMEM((load, chans), f32),
+            pltpu.VMEM((LOADERS, NX, load, chans), f32),
             pltpu.VMEM((CORES, LOADERS, load, chans), f32),
             pltpu.VMEM((frames_n + PIECE, chans), f32),
             pltpu.VMEM((frames_n + PIECE, chans), f32),
             pltpu.VMEM((frames_n, chans), f32),
             pltpu.VMEM((frames_n, chans), f32),
-            pltpu.VMEM((frames_n, rows // 2, half, chans), bf16),
             pltpu.SMEM((2,), jnp.int32),
             pltpu.VMEM((1, chans), f32),
             pltpu.VMEM((1, chans), f32),
@@ -343,13 +320,11 @@
             dma((pieces,)),
             dma((4,)),
             dma((3,)),
-            dma((2,)),
-            dma((13,)),
+            dma((25,)),
             dma((pieces,)),
-            dma((2,)),
-            dma((NZ,)),
-            dma((NX,)),
-            dma((LOADERS,)),
+            dma((NZ, CORES)),
+            dma((LOADERS, NX)),
+            dma((1,)),
             dma((2,)),
             dma((pieces,)),
         ],

time: 33.7 us -> 30.4 us (0.902)
  Pallas kernels: 31.3 us -> 29.3 us
  local copies, waits for them, and re-layouts: 2.26 us -> 0.97 us
    pallas_call x1, Pallas kernels: 31.3 us -> 29.3 us  [local(): pl.pallas_call(kernel, out_shape=pltpu.VMEM((frames_n, rows // 2, half, c...]
    unnamed x1, local copies, waits for them, and re-layouts: 2.26 us -> 0.97 us
where the time goes in v4:
time: 30.4 us; the launch traced here: 30.3 us
  Pallas kernels  29.3 us (96%)
  local copies, waits for them, and re-layouts  0.97 us (3%)
    pallas_call x1, Pallas kernels, local(): pl.pallas_call(kernel, out_shape=pltpu.VMEM((frames_n, rows // 2, half, c...  29.3 us
    unnamed x1, local copies, waits for them, and re-layouts  0.97 us

profile of v4, /device:TPU:1, one launch (start us, length us, event | category | flops | bytes accessed | tf_op | source)
XLA Modules:
  0.0 30.3 jit_solution(14073072264165593777)
XLA Ops:
  0.0 29.3 %shard_map.64 = bf16[64,2,32,128]{3,2,1,0:T(8,128)(2,1)S(1)} custom-call(bf16[64,4,64,128]{3,2,1,0:T(8,128)(2,1)} %frames.1, s32[2]{0:T(128)} %clips.1, f32[1,128]{1,0:T(1,128)} %bitcast.3, f32[1,128]{1,0:T(1,128)} %bitcast.4, bf16[3,3,3,128,128]{4,3,2,1,0:T(8,128)(2,1)} %weight.1, f32[1,128]{1,0:T(1,128)} %bitcast.5), custom_call_target="tpu_custom_call" | custom-call | tf_op jit(solution)/shard_map/pallas_call | solution.py:296
  29.3 1.0 %copy.8 = bf16[64,2,32,128]{3,2,1,0:T(8,128)(2,1)} copy(bf16[64,2,32,128]{3,2,1,0:T(8,128)(2,1)S(1)} %shard_map.64) | data formatting | bytes 2097152

commit v5 on v4

--- a/solution.py
+++ b/solution.py
@@ -12,8 +12,9 @@
 ENCS = NX * NZ * CORES
 PIECE = 8
 CHUNK = 8
-EARLY = 2
+EARLY = 1
 BARRIER_AT = 4
+WAIT = 2
 
 
 def spread(values, lane, at):
@@ -49,11 +50,6 @@
     plane = [(i, j) for i in range(LOADERS) for j in range(NX) if (i, j) != (0, 0)]
     plane_devices = [((l + i) % LOADERS, enc_at((xi + j) % NX, z, c)) for i, j in plane]
 
-    barrier = pltpu.get_barrier_semaphore()
-    senders = column_devices + plane_devices + [(l, e_prev), (l_prev, e_prev)]
-    for device in senders:
-        pl.semaphore_signal(barrier, inc=1, device_id=device, device_id_type=MESH)
-
     loads = []
     for i in range(pieces):
         loads.append(
@@ -72,13 +68,16 @@
     ]
     for copy in smalls:
         copy.start()
+    barrier = pltpu.get_barrier_semaphore()
+    senders = column_devices + plane_devices + [(l, e_prev), (l_prev, e_prev)]
+    for device in senders:
+        pl.semaphore_signal(barrier, inc=1, device_id=device, device_id_type=MESH)
+
     weights = [
         pltpu.make_async_copy(weight.at[:, :, 1], w.at[:, :, pl.ds(0, chans), pl.ds(0, chans)], w_sem.at[0]),
         pltpu.make_async_copy(weight.at[:, :, 2], w.at[:, :, pl.ds(chans, chans), pl.ds(0, chans)], w_sem.at[1]),
         pltpu.make_async_copy(weight.at[:, :, 0], w.at[:, :, pl.ds(chans, chans), pl.ds(chans, chans)], w_sem.at[2]),
     ]
-    for copy in weights:
-        copy.start()
 
     def remote(src, dst, sent, recv, device):
         return pltpu.make_async_remote_copy(
@@ -114,26 +113,39 @@
             start(sent)
             start(halos[:EARLY])
         loads[i].wait()
-        values = x[pl.ds(2 + i * PIECE, PIECE), pl.ds(1, rows)].astype(jnp.float32)
-        first = jnp.sum(values, axis=(1, 2))
-        second = jnp.sum(values * values, axis=(1, 2))
-        for by in (1, 2):
-            first = first + pltpu.roll(first, chans - by, axis=1)
-            second = second + pltpu.roll(second, chans - by, axis=1)
-        second = pltpu.roll(second, 1, axis=1)
-        sums.append(jnp.where(role == 0, first, jnp.where(role == 1, second, 0.0)))
+        first, second = [], []
+        for f in range(PIECE):
+            tiles = x[2 + i * PIECE + f, pl.ds(1, rows)].astype(jnp.float32).reshape(rows * cols // 8, 8, chans)
+            one, two = [tiles[n] for n in range(4)], [tiles[n] * tiles[n] for n in range(4)]
+            for n in range(4, rows * cols // 8):
+                one[n % 4] = one[n % 4] + tiles[n]
+                two[n % 4] = two[n % 4] + tiles[n] * tiles[n]
+            first.append((one[0] + one[1]) + (one[2] + one[3]))
+            second.append((two[0] + two[1]) + (two[2] + two[3]))
+        first = jnp.sum(jnp.stack(first), axis=1)
+        second = jnp.sum(jnp.stack(second), axis=1)
+        sums.append(
+            jnp.where(
+                lane % 2 == 0, first + pltpu.roll(first, chans - 1, axis=1), second + pltpu.roll(second, 1, axis=1)
+            )
+        )
     smalls[0].wait()
-    id_lane = (l % 2) * frames_n + 2 * e
+    share = frames_n // CORES
+    id_lane = l * share + (2 * e) % share
     ids = jnp.where(
         lane == id_lane,
         (ids_s[0] + 1).astype(jnp.float32),
         jnp.where(lane == id_lane + 1, (ids_s[1] + 1).astype(jnp.float32), 0.0),
-    )
+    )[:1]
     for core in range(CORES):
         for block in range(2):
             at = 4 * core + block
-            part[core, pl.ds(block * PIECE, PIECE)] = sums[at] + pltpu.roll(sums[at + 2], 2, axis=1)
-        part[core, pl.ds(2 * PIECE, 1)] = ids[:1]
+            near, far = sums[at], sums[at + 2]
+            part[core, pl.ds(block * PIECE, PIECE)] = jnp.where(
+                role < 2, near + pltpu.roll(near, chans - 2, axis=1), far + pltpu.roll(far, 2, axis=1)
+            )
+        for owner in range(CORES):
+            part[core, pl.ds(2 * PIECE + owner, 1)] = jnp.where(2 * e // share == owner, ids, 0.0)
 
     def divide(frame):
         for row in range(1, rows + 1):
@@ -153,6 +165,7 @@
     for n, ((i, j), device) in enumerate(zip(column, column_devices)):
         sent.append(remote(part.at[(c + j) % CORES], from_chips.at[z, c], send_sem.at[2 + n], recv_chips.at[z, c], device))
         sent[-1].start()
+    start(weights)
     w[:, :, :chans, chans:] = jnp.zeros((3, 3, chans, chans), jnp.bfloat16)
     from_chips[z, c] = part[c]
     steps = frames_n // 4
@@ -178,31 +191,41 @@
     to_core = remote(table.at[c], table.at[c], send_sem.at[24], recv_core.at[0], other_core)
     to_core.start()
     sent.append(to_core)
+    count = frames_n + PIECE
+    at_row = lax.broadcasted_iota(jnp.int32, (count, chans), 0) + (l * frames_n - PIECE)
+    place = lax.broadcasted_iota(jnp.int32, (count, chans), 1)
+    frame_of = [(place // share) * frames_n + core * share + place % share for core in range(CORES)]
+    id_of = []
+    for core in range(CORES):
+        row = table[c, 0, pl.ds(2 * PIECE + core, 1)]
+        for loader in range(1, LOADERS):
+            row = row + table[c, loader, pl.ds(2 * PIECE + core, 1)]
+        id_of.append(jnp.broadcast_to(row, (count, chans)))
+
+    def id_before(by):
+        found = sum(jnp.where(at == at_row - by, row, 0.0) for at, row in zip(frame_of, id_of))
+        return jnp.sum(found, axis=1, keepdims=True)
+
+    own = id_before(0)
+    for keep, by in ((keep1, 1), (keep2, 2)):
+        kept = jnp.where(id_before(by) == own, 1.0, 0.0)
+        keep[...] = jnp.broadcast_to(kept[PIECE:], (frames_n, chans))
+    members = [jnp.where((row == own) & (at <= at_row), 1.0, 0.0) for at, row in zip(frame_of, id_of)]
+
+    def half_of_run(core):
+        blocks = []
+        for loader in range(LOADERS):
+            block = table[core, loader, pl.ds(0, 2 * PIECE)]
+            blocks += [block, pltpu.roll(block, chans - 2, axis=1)]
+        sums_of = jnp.where(place[:1] % GROUP == 3, 1.0, jnp.concatenate(blocks, axis=0))
+        member = jnp.where(core == 0, members[0], members[1])
+        return jnp.dot(member, sums_of, precision=lax.Precision.HIGHEST, preferred_element_type=jnp.float32)
+
+    run = half_of_run(c)
     for copy in smalls[1:] + weights:
         copy.wait()
     arrived(table.at[1 - c], recv_core.at[0])
-
-    total, count = LOADERS * frames_n, frames_n + PIECE
-    blocks = []
-    for loader in range(LOADERS):
-        for core in range(CORES):
-            block = table[core, loader, pl.ds(0, 2 * PIECE)]
-            blocks += [block, pltpu.roll(block, chans - 2, axis=1)]
-    everything = jnp.concatenate(blocks, axis=0)
-    lane_all = lax.broadcasted_iota(jnp.int32, (total, chans), 1) % GROUP
-    everything = jnp.where(lane_all == 3, 1.0, everything)
-    id_row = [table[0, loader, pl.ds(2 * PIECE, 1)] for loader in range(LOADERS)]
-    id_row = jnp.concatenate([id_row[0] + id_row[1], id_row[2] + id_row[3]], axis=1)
-    id_row = jnp.broadcast_to(id_row, (count, total))
-    at_col = lax.broadcasted_iota(jnp.int32, (count, total), 1)
-    at_row = lax.broadcasted_iota(jnp.int32, (count, total), 0) + (l * frames_n - PIECE)
-
-    def id_before(by):
-        return jnp.sum(jnp.where(at_col == at_row - by, id_row, 0.0), axis=1, keepdims=True)
-
-    own = id_before(0)
-    member = jnp.where((id_row == own) & (at_col <= at_row), 1.0, 0.0)
-    run = jnp.dot(member, everything, precision=lax.Precision.HIGHEST, preferred_element_type=jnp.float32)
+    run = run + half_of_run(1 - c)
     lane_run = lax.broadcasted_iota(jnp.int32, (count, chans), 1)
     per = jnp.maximum(spread(run, lane_run, 3), 1.0) * float(ENCS * rows * cols * GROUP)
     mean = spread(run, lane_run, 0) / per
@@ -210,10 +233,6 @@
     times = lax.rsqrt(var + EPS) * gain_v[...]
     scale[...] = 0.5 * times
     shift[...] = 0.5 * (bias_v[...] - mean * times)
-    for keep, by in ((keep1, 1), (keep2, 2)):
-        kept = jnp.where(id_before(by) == own, 1.0, 0.0)
-        keep[...] = jnp.broadcast_to(kept[PIECE:], (frames_n, chans))
-
     def silu_of(value, frame):
         at = pl.ds(frame + PIECE - 2, 1)
         s, b = scale[at], shift[at]
@@ -266,8 +285,10 @@
             activate_chunk(i + 1)
         convolve(i, 1)
 
-    for piece in range(pieces):
-        arrived(x.at[pl.ds(2 + piece * PIECE, PIECE), 0], recv_halo.at[piece])
+    def await_halo(first, last):
+        for piece in range(first, last):
+            arrived(x.at[pl.ds(2 + piece * PIECE, PIECE), 0], recv_halo.at[piece])
+
     arrived(x.at[pl.ds(0, 2), 0], recv_frames.at[1])
 
     def activate_halo_chunk(i):
@@ -276,9 +297,12 @@
 
     for frame in range(2):
         activate_halo(frame, frame)
+    await_halo(0, WAIT)
     activate_halo_chunk(0)
     for i in range(chunks):
         if i + 1 < chunks:
+            if (i + 1) % WAIT == 0:
+                await_halo(i + 1, min(i + 1 + WAIT, pieces))
             activate_halo_chunk(i + 1)
         convolve(i, 0)
 
@@ -292,7 +316,7 @@
     pieces, chunks = frames_n // PIECE, frames_n // CHUNK
     f32, bf16 = jnp.float32, jnp.bfloat16
     dma = pltpu.SemaphoreType.DMA
-    load = 2 * PIECE + 1
+    load = 2 * PIECE + CORES
     return pl.pallas_call(
         kernel,
         out_shape=pltpu.VMEM((frames_n, rows // 2, half, chans), bf16),

time: 30.4 us -> 29.8 us (0.980)
  Pallas kernels: 29.3 us -> 28.7 us
    pallas_call x1, Pallas kernels: 29.3 us -> 28.7 us  [local(): pl.pallas_call(kernel, out_shape=pltpu.VMEM((frames_n, rows // 2, half, c...]
where the time goes in v5:
time: 29.8 us; the launch traced here: 29.7 us
  Pallas kernels  28.7 us (96%)
  local copies, waits for them, and re-layouts  0.97 us (3%)
    pallas_call x1, Pallas kernels, local(): pl.pallas_call(kernel, out_shape=pltpu.VMEM((frames_n, rows // 2, half, c...  28.7 us
    unnamed x1, local copies, waits for them, and re-layouts  0.97 us

profile of v5, /device:TPU:1, one launch (start us, length us, event | category | flops | bytes accessed | tf_op | source)
XLA Modules:
  0.0 29.7 jit_solution(13935706321548351504)
XLA Ops:
  0.0 28.7 %shard_map.64 = bf16[64,2,32,128]{3,2,1,0:T(8,128)(2,1)S(1)} custom-call(bf16[64,4,64,128]{3,2,1,0:T(8,128)(2,1)} %frames.1, s32[2]{0:T(128)} %clips.1, f32[1,128]{1,0:T(1,128)} %bitcast.3, f32[1,128]{1,0:T(1,128)} %bitcast.4, bf16[3,3,3,128,128]{4,3,2,1,0:T(8,128)(2,1)} %weight.1, f32[1,128]{1,0:T(1,128)} %bitcast.5), custom_call_target="tpu_custom_call" | custom-call | tf_op jit(solution)/shard_map/pallas_call | solution.py:320
  28.7 1.0 %copy.8 = bf16[64,2,32,128]{3,2,1,0:T(8,128)(2,1)} copy(bf16[64,2,32,128]{3,2,1,0:T(8,128)(2,1)S(1)} %shard_map.64) | data formatting | bytes 2097152

commit v6 on v5

--- a/solution.py
+++ b/solution.py
@@ -46,8 +46,10 @@
     e_next, e_prev = (e + 1) % ENCS, (e + ENCS - 1) % ENCS
     other_core = (l, enc_at(xi, z, 1 - c))
     column = [(i, j) for i in range(NZ) for j in range(CORES) if (i, j) != (0, 0)]
+    column.sort(key=lambda at: (-min(at[0], NZ - at[0]), -at[1]))
     column_devices = [(l, enc_at(xi, (z + i) % NZ, (c + j) % CORES)) for i, j in column]
     plane = [(i, j) for i in range(LOADERS) for j in range(NX) if (i, j) != (0, 0)]
+    plane.sort(key=lambda at: -min(at[0], LOADERS - at[0]) - min(at[1], NX - at[1]))
     plane_devices = [((l + i) % LOADERS, enc_at((xi + j) % NX, z, c)) for i, j in plane]
 
     loads = []

time: 29.8 us -> 29.3 us (0.983)
  Pallas kernels: 28.7 us -> 28.2 us
    pallas_call x1, Pallas kernels: 28.7 us -> 28.2 us  [local(): pl.pallas_call(kernel, out_shape=pltpu.VMEM((frames_n, rows // 2, half, c...]
where the time goes in v6:
time: 29.3 us; the launch traced here: 29.2 us
  Pallas kernels  28.2 us (96%)
  local copies, waits for them, and re-layouts  0.97 us (3%)
    pallas_call x1, Pallas kernels, local(): pl.pallas_call(kernel, out_shape=pltpu.VMEM((frames_n, rows // 2, half, c...  28.2 us
    unnamed x1, local copies, waits for them, and re-layouts  0.97 us

profile of v6, /device:TPU:1, one launch (start us, length us, event | category | flops | bytes accessed | tf_op | source)
XLA Modules:
  0.0 29.2 jit_solution(11702283684818206621)
XLA Ops:
  0.0 28.2 %shard_map.64 = bf16[64,2,32,128]{3,2,1,0:T(8,128)(2,1)S(1)} custom-call(bf16[64,4,64,128]{3,2,1,0:T(8,128)(2,1)} %frames.1, s32[2]{0:T(128)} %clips.1, f32[1,128]{1,0:T(1,128)} %bitcast.3, f32[1,128]{1,0:T(1,128)} %bitcast.4, bf16[3,3,3,128,128]{4,3,2,1,0:T(8,128)(2,1)} %weight.1, f32[1,128]{1,0:T(1,128)} %bitcast.5), custom_call_target="tpu_custom_call" | custom-call | tf_op jit(solution)/shard_map/pallas_call | solution.py:322
  28.2 1.0 %copy.8 = bf16[64,2,32,128]{3,2,1,0:T(8,128)(2,1)} copy(bf16[64,2,32,128]{3,2,1,0:T(8,128)(2,1)S(1)} %shard_map.64) | data formatting | bytes 2097152
